TPU v7x, 32 devices: a whole 2x2x4 slice. The times are simulated.
32 devices in a mesh: groups: 2 (over x), path: 8 (over z, y), cons: 2 (over core).
Axes of the slice: x: 2, y: 2, z: 4, core: 2. Of those that a mesh axis runs over, the one named last changes fastest.
Arguments:
- tile_values: bfloat16 [16, 2, 32, 128, 128], P(('groups', 'path'), 'cons'), parts along dimension 0, may hold values from -0.125 to 0.125
- row_blocks: int32 [16, 2, 32], P(('groups', 'path'), 'cons'), parts along dimension 0, may hold values from 0 to 15, as said below
- col_blocks: int32 [16, 2, 32], P(('groups', 'path'), 'cons'), parts along dimension 0, may hold values from 0 to 7
- path_cost: float32 [16384], P(('groups', 'path', 'cons')), parts along dimension 0, may hold values from -6 to 6
- path_bound: float32 [16384], P(('groups', 'path', 'cons')), parts along dimension 0, may hold values from 0.5 to 2
- primal_start: float32 [16384], P(('groups', 'path', 'cons')), parts along dimension 0, may hold values from 0 to 1
- dual_start: float32 [8192], P(('groups', 'path', 'cons')), parts along dimension 0, may hold values from 0 to 1
- row_limits: float32 [8192], P(('groups', 'path', 'cons')), parts along dimension 0, may hold values from -6 to 6
- step_size: float32 [2], P('groups'), parts along dimension 0, may hold values from 0.3 to 0.45
- weight_start: float32 [2], P('groups'), parts along dimension 0, may hold values from 0.5 to 2
- restart_flags: int32 [12], P('groups'), parts along dimension 0, may hold values from 0 to 1
Outputs:
- primal_out: float32 [16384], P(('groups', 'path', 'cons')), parts along dimension 0
- dual_out: float32 [8192], P(('groups', 'path', 'cons')), parts along dimension 0
- link_loads: float32 [8192], P(('groups', 'path', 'cons')), parts along dimension 0
There are 2 independent parts, one for each index of `groups`. A program takes and returns all parts, laid end to end along the dimension named above; each array names one. Nothing has to cross between parts.
Inputs may be any that keep to these rules, and one draw needn't show every extreme that they name: `row_blocks`: row block of a tile inside its constraint half; for every device and every index o of path, at most 8 of the device's tiles lie in row blocks 2 * o to 2 * o + 1, and on every device some index o has exactly 8.
All inputs are finite; a program needn't handle non-finite values.
Results may differ from a plain program's by a relative error of at most 0.0031.
Values may be sent and summed in bfloat16 or wider, within the bound.
A program may use at most 64 MiB of HBM per device.

v0:
```python
import jax
import jax.numpy as jnp
from jax import lax
from jax.sharding import PartitionSpec as P


def tile_rows(tile_values, col_blocks, primal_low):
    blocks = primal_low.reshape(-1, tile_values.shape[-1])
    picked = blocks[col_blocks]
    return jnp.einsum("tij,tj->ti", tile_values, picked, preferred_element_type=jnp.float32)


def col_partial(tile_values, picked, col_blocks, col_count):
    products = jnp.einsum("tij,ti->tj", tile_values, picked, preferred_element_type=jnp.float32)
    return jax.ops.segment_sum(products, col_blocks, num_segments=col_count).reshape(-1)


def shards(
    tile_values,
    row_blocks,
    col_blocks,
    path_cost,
    path_bound,
    primal_start,
    dual_start,
    row_limits,
    step_size,
    weight_start,
    restart_flags,
):
    epsilon = 1e-06
    tile_values = tile_values[0, 0]
    row_blocks = row_blocks[0, 0]
    col_blocks = col_blocks[0, 0]
    edge = tile_values.shape[-1]
    primal_width = path_cost.shape[0]
    dual_width = row_limits.shape[0]
    col_count = primal_width * lax.axis_size("cons") // edge
    own_blocks = dual_width // edge
    path_count = lax.axis_size("path")
    tile_count = row_blocks.shape[0]
    capacity = max(2, (2 * tile_count + path_count - 1) // path_count)
    primal_now = primal_start
    dual_now = dual_start
    owners = row_blocks // own_blocks
    positions = jnp.arange(tile_count, dtype=jnp.int32)
    earlier = (owners[:, None] == owners[None, :]) & (positions[None, :] < positions[:, None])
    ranks = jnp.sum(earlier.astype(jnp.int32), axis=1)
    targets = owners * capacity + ranks
    slot_rows = (
        jnp.full((path_count * capacity,), -1, jnp.int32).at[targets].set(row_blocks % own_blocks)
    )
    arrived = lax.all_to_all(slot_rows, "path", split_axis=0, concat_axis=0, tiled=True)
    selector = (arrived[None, :] == jnp.arange(own_blocks, dtype=jnp.int32)[:, None]).astype(
        jnp.float32
    )
    reply_rows = jnp.maximum(arrived, 0)

    def primal_product(primal_low):
        primal_low = lax.all_gather(primal_low, "cons", axis=0, tiled=True)
        products = tile_rows(tile_values, col_blocks, primal_low)
        outgoing = jnp.zeros((path_count * capacity, edge), jnp.float32).at[targets].set(products)
        incoming = lax.all_to_all(outgoing, "path", split_axis=0, concat_axis=0, tiled=True)
        return jnp.dot(selector, incoming, precision=lax.Precision.HIGHEST).reshape(-1)

    anchor_primal = primal_now
    anchor_dual = dual_now
    primal_sum = jnp.zeros_like(primal_now)
    dual_sum = jnp.zeros_like(dual_now)
    steps_taken = jnp.zeros((), jnp.float32)
    eta = step_size[0]
    weight = weight_start[0]
    for turn_index in range(restart_flags.shape[0]):
        dual_low = dual_now.astype(jnp.bfloat16)
        replies = dual_low.reshape(own_blocks, edge)[reply_rows]
        returned = lax.all_to_all(replies, "path", split_axis=0, concat_axis=0, tiled=True)
        picked = returned[targets]
        partial_terms = col_partial(tile_values, picked, col_blocks, col_count)
        gradient = lax.psum_scatter(partial_terms, "cons", scatter_dimension=0, tiled=True)
        primal_next = jnp.clip(primal_now - eta / weight * (path_cost + gradient), 0.0, path_bound)
        extrapolated = (2.0 * primal_next - primal_now).astype(jnp.bfloat16)
        activity = primal_product(extrapolated)
        dual_next = jnp.maximum(dual_now + eta * weight * (activity - row_limits), 0.0)
        primal_sum = primal_sum + primal_next
        dual_sum = dual_sum + dual_next
        steps_taken = steps_taken + 1.0
        primal_mean = primal_sum / steps_taken
        dual_mean = dual_sum / steps_taken
        primal_shift = primal_mean - anchor_primal
        dual_shift = dual_mean - anchor_dual
        primal_move, dual_move = lax.psum(
            (jnp.sum(primal_shift * primal_shift), jnp.sum(dual_shift * dual_shift)),
            ("path", "cons"),
        )
        candidate = jnp.sqrt(
            weight * jnp.sqrt(dual_move + epsilon) / jnp.sqrt(primal_move + epsilon)
        )
        restart = restart_flags[turn_index] == 1
        primal_now = jnp.where(restart, primal_mean, primal_next)
        dual_now = jnp.where(restart, dual_mean, dual_next)
        anchor_primal = jnp.where(restart, primal_mean, anchor_primal)
        anchor_dual = jnp.where(restart, dual_mean, anchor_dual)
        primal_sum = jnp.where(restart, jnp.zeros_like(primal_sum), primal_sum)
        dual_sum = jnp.where(restart, jnp.zeros_like(dual_sum), dual_sum)
        steps_taken = jnp.where(restart, jnp.zeros((), jnp.float32), steps_taken)
        weight = jnp.where(restart, candidate, weight)
    loads = primal_product(primal_now.astype(jnp.bfloat16))
    return (primal_now, dual_now, loads)


def solution(mesh):
    in_specs = (
        P(("groups", "path"), "cons", None, None, None),
        P(("groups", "path"), "cons", None),
        P(("groups", "path"), "cons", None),
        P(("groups", "path", "cons")),
        P(("groups", "path", "cons")),
        P(("groups", "path", "cons")),
        P(("groups", "path", "cons")),
        P(("groups", "path", "cons")),
        P("groups"),
        P("groups"),
        P("groups"),
    )
    out_specs = (
        P(("groups", "path", "cons")),
        P(("groups", "path", "cons")),
        P(("groups", "path", "cons")),
    )
    return jax.shard_map(shards, mesh=mesh, in_specs=in_specs, out_specs=out_specs, check_vma=False)
```

profile of v0, /device:TPU:0, one launch (start us, length us, event | category | flops | bytes accessed | tf_op | source)
XLA Modules:
  0.0 356.9 jit_solution(11803322861526937581)
XLA Ops:
  3.4 7.4 %all-to-all-start = ((s32[8,8,1]{1,2,0:T(1,128)}), s32[8,8,1]{1,2,0:T(1,128)S(1)}, u32[]{:S(2)}, u32[]{:S(2)}) async-start(s32[8,8,1]{1,2,0:T(1,128)} %bitcast.14), calls=%async_computation | async-start | bytes 8192 | tf_op jit(solution)/shard_map/all_to_all | solution.py:53
  11.5 5.8 %all-to-all-done = s32[8,8,1]{1,2,0:T(1,128)S(1)} async-done(((s32[8,8,1]{1,2,0:T(1,128)}), s32[8,8,1]{1,2,0:T(1,128)S(1)}, u32[]{:S(2)}, u32[]{:S(2)}) %all-to-all-start) | async-done | bytes 288 | tf_op jit(solution)/shard_map/all_to_all | solution.py:53
  19.8 3.3 all-to-all-start.1
  38.8 3.3 all-to-all-start.2
  42.3 6.5 %all-to-all-done.2 = f32[8,8,128]{2,1,0:T(8,128)S(1)} async-done(((f32[8,8,128]{2,1,0:T(8,128)}), f32[8,8,128]{2,1,0:T(8,128)S(1)}, u32[]{:S(2)}, u32[]{:S(2)}) %all-to-all-start.2) | async-done | bytes 32800 | tf_op jit(solution)/shard_map/all_to_all | solution.py:63
  50.8 3.5 all-to-all-start.3
  55.5 33.1 %all-reduce.10 = (f32[]{:T(128)}, f32[]{:T(128)}) all-reduce(f32[]{:T(128)} %get-tuple-element.40, f32[]{:T(128)} %get-tuple-element.33), channel_id=1, replica_groups=mesh['groups'=2,'path'=8,'cons'=2] {'path','cons'}, use_global_device_ids=true, to_apply=%region_6.7 | all-reduce | flops 2 | bytes 16 | tf_op jit(solution)/shard_map/psum | solution.py:91
  99.2 3.3 all-to-all-start.4
  103.2 5.9 %all-to-all-done.4 = f32[8,8,128]{2,1,0:T(8,128)S(1)} async-done(((f32[8,8,128]{2,1,0:T(8,128)}), f32[8,8,128]{2,1,0:T(8,128)S(1)}, u32[]{:S(2)}, u32[]{:S(2)}) %all-to-all-start.4) | async-done | bytes 32800 | tf_op jit(solution)/shard_map/all_to_all | solution.py:63
  111.1 3.3 all-to-all-start.5
  114.5 33.1 %all-reduce.9 = (f32[]{:T(128)}, f32[]{:T(128)}) all-reduce(f32[]{:T(128)} %get-tuple-element.31, f32[]{:T(128)} %get-tuple-element.29), channel_id=1, replica_groups=mesh['groups'=2,'path'=8,'cons'=2] {'path','cons'}, use_global_device_ids=true, to_apply=%region_13.14 | all-reduce | flops 2 | bytes 16 | tf_op jit(solution)/shard_map/psum | solution.py:91
  158.2 3.3 all-to-all-start.6
  162.2 6.0 %all-to-all-done.6 = f32[8,8,128]{2,1,0:T(8,128)S(1)} async-done(((f32[8,8,128]{2,1,0:T(8,128)}), f32[8,8,128]{2,1,0:T(8,128)S(1)}, u32[]{:S(2)}, u32[]{:S(2)}) %all-to-all-start.6) | async-done | bytes 32800 | tf_op jit(solution)/shard_map/all_to_all | solution.py:63
  170.2 3.3 all-to-all-start.7
  173.5 33.1 %all-reduce.8 = (f32[]{:T(128)}, f32[]{:T(128)}) all-reduce(f32[]{:T(128)} %get-tuple-element.25, f32[]{:T(128)} %get-tuple-element.21), channel_id=1, replica_groups=mesh['groups'=2,'path'=8,'cons'=2] {'path','cons'}, use_global_device_ids=true, to_apply=%region_20.21 | all-reduce | flops 2 | bytes 16 | tf_op jit(solution)/shard_map/psum | solution.py:91
  217.2 3.3 all-to-all-start.8
  221.2 6.0 %all-to-all-done.8 = f32[8,8,128]{2,1,0:T(8,128)S(1)} async-done(((f32[8,8,128]{2,1,0:T(8,128)}), f32[8,8,128]{2,1,0:T(8,128)S(1)}, u32[]{:S(2)}, u32[]{:S(2)}) %all-to-all-start.8) | async-done | bytes 32800 | tf_op jit(solution)/shard_map/all_to_all | solution.py:63
  232.5 33.1 %all-reduce.7 = (f32[]{:T(128)}, f32[]{:T(128)}) all-reduce(f32[]{:T(128)} %get-tuple-element.19, f32[]{:T(128)} %get-tuple-element.17), channel_id=1, replica_groups=mesh['groups'=2,'path'=8,'cons'=2] {'path','cons'}, use_global_device_ids=true, to_apply=%region_27.28 | all-reduce | flops 2 | bytes 16 | tf_op jit(solution)/shard_map/psum | solution.py:91
  276.3 3.3 all-to-all-start.10
  280.2 6.0 %all-to-all-done.10 = f32[8,8,128]{2,1,0:T(8,128)S(1)} async-done(((f32[8,8,128]{2,1,0:T(8,128)}), f32[8,8,128]{2,1,0:T(8,128)S(1)}, u32[]{:S(2)}, u32[]{:S(2)}) %all-to-all-start.10) | async-done | bytes 32800 | tf_op jit(solution)/shard_map/all_to_all | solution.py:63
  288.2 3.3 all-to-all-start.11
  292.2 33.2 %all-reduce.6 = (f32[]{:T(128)}, f32[]{:T(128)}) all-reduce(f32[]{:T(128)} %get-tuple-element.38, f32[]{:T(128)} %get-tuple-element.36), channel_id=1, replica_groups=mesh['groups'=2,'path'=8,'cons'=2] {'path','cons'}, use_global_device_ids=true, to_apply=%region_34.35 | all-reduce | flops 2 | bytes 16 | tf_op jit(solution)/shard_map/psum | solution.py:91
  345.9 3.6 %all-to-all-start.12 = ((f32[8,8,128]{2,1,0:T(8,128)}), f32[8,8,128]{2,1,0:T(8,128)S(1)}, u32[]{:S(2)}, u32[]{:S(2)}) async-start(f32[8,8,128]{2,1,0:T(8,128)} %bitcast.92), calls=%async_computation.12 | async-start | bytes 65536 | tf_op jit(solution)/shard_map/all_to_all | solution.py:63
  350.2 6.0 %all-to-all-done.12 = f32[8,8,128]{2,1,0:T(8,128)S(1)} async-done(((f32[8,8,128]{2,1,0:T(8,128)}), f32[8,8,128]{2,1,0:T(8,128)S(1)}, u32[]{:S(2)}, u32[]{:S(2)}) %all-to-all-start.12) | async-done | bytes 32800 | tf_op jit(solution)/shard_map/all_to_all | solution.py:63
  (146 shorter events, 90.6 us)
Async XLA Ops:
  0.6 29.6 %copy-start = (bf16[1,1,32,128,128]{4,3,2,1,0:T(8,128)(2,1)S(1)}, bf16[1,1,32,128,128]{4,3,2,1,0:T(8,128)(2,1)}, u32[]{:S(2)}) copy-start(bf16[1,1,32,128,128]{4,3,2,1,0:T(8,128)(2,1)} %param.11) | copy-start | bytes 3145732
  1.4 0.7 copy-start.7
  3.4 7.4 %copy-start.6 = (f32[256]{0:T(256)S(1)}, f32[256]{0:T(256)}, u32[]{:S(2)}) copy-start(f32[256]{0:T(256)} %param.17) | copy-start | bytes 3076
  3.4 13.9 %all-to-all-start = ((s32[8,8,1]{1,2,0:T(1,128)}), s32[8,8,1]{1,2,0:T(1,128)S(1)}, u32[]{:S(2)}, u32[]{:S(2)}) async-start(s32[8,8,1]{1,2,0:T(1,128)} %bitcast.14), calls=%async_computation | async-start | bytes 8192 | tf_op jit(solution)/shard_map/all_to_all | solution.py:53
  10.8 0.7 copy-start.8
  19.8 9.9 %all-to-all-start.1 = ((bf16[8,8,128]{2,1,0:T(8,128)(2,1)}), bf16[8,8,128]{2,1,0:T(8,128)(2,1)S(1)}, u32[]{:S(2)}, u32[]{:S(2)}) async-start(bf16[8,8,128]{2,1,0:T(8,128)(2,1)} %bitcast.15), calls=%async_computation.1 | async-start | bytes 32768 | tf_op jit(solution)/shard_map/all_to_all | solution.py:76
  24.5 0.7 copy-start.9
  31.4 2.5 copy-start.1
  31.4 2.5 copy-start.2
  31.4 2.5 copy-start.3
  38.8 10.0 %all-to-all-start.2 = ((f32[8,8,128]{2,1,0:T(8,128)}), f32[8,8,128]{2,1,0:T(8,128)S(1)}, u32[]{:S(2)}, u32[]{:S(2)}) async-start(f32[8,8,128]{2,1,0:T(8,128)} %bitcast.27), calls=%async_computation.2 | async-start | bytes 65536 | tf_op jit(solution)/shard_map/all_to_all | solution.py:63
  42.2 6.6 %copy-start.4 = (f32[256]{0:T(256)S(1)}, f32[256]{0:T(256)}, u32[]{:S(2)}) copy-start(f32[256]{0:T(256)} %param.18) | copy-start | bytes 3076
  50.8 3.5 copy-start.5
  50.8 39.3 %all-to-all-start.3 = ((bf16[8,8,128]{2,1,0:T(8,128)(2,1)}), bf16[8,8,128]{2,1,0:T(8,128)(2,1)S(1)}, u32[]{:S(2)}, u32[]{:S(2)}) async-start(bf16[8,8,128]{2,1,0:T(8,128)(2,1)} %bitcast.31), calls=%async_computation.3 | async-start | bytes 32768 | tf_op jit(solution)/shard_map/all_to_all | solution.py:76
  99.2 10.0 %all-to-all-start.4 = ((f32[8,8,128]{2,1,0:T(8,128)}), f32[8,8,128]{2,1,0:T(8,128)S(1)}, u32[]{:S(2)}, u32[]{:S(2)}) async-start(f32[8,8,128]{2,1,0:T(8,128)} %bitcast.40), calls=%async_computation.4 | async-start | bytes 65536 | tf_op jit(solution)/shard_map/all_to_all | solution.py:63
  111.1 37.9 %all-to-all-start.5 = ((bf16[8,8,128]{2,1,0:T(8,128)(2,1)}), bf16[8,8,128]{2,1,0:T(8,128)(2,1)S(1)}, u32[]{:S(2)}, u32[]{:S(2)}) async-start(bf16[8,8,128]{2,1,0:T(8,128)(2,1)} %bitcast.44), calls=%async_computation.5 | async-start | bytes 32768 | tf_op jit(solution)/shard_map/all_to_all | solution.py:76
  158.2 10.0 %all-to-all-start.6 = ((f32[8,8,128]{2,1,0:T(8,128)}), f32[8,8,128]{2,1,0:T(8,128)S(1)}, u32[]{:S(2)}, u32[]{:S(2)}) async-start(f32[8,8,128]{2,1,0:T(8,128)} %bitcast.53), calls=%async_computation.6 | async-start | bytes 65536 | tf_op jit(solution)/shard_map/all_to_all | solution.py:63
  170.2 37.9 %all-to-all-start.7 = ((bf16[8,8,128]{2,1,0:T(8,128)(2,1)}), bf16[8,8,128]{2,1,0:T(8,128)(2,1)S(1)}, u32[]{:S(2)}, u32[]{:S(2)}) async-start(bf16[8,8,128]{2,1,0:T(8,128)(2,1)} %bitcast.57), calls=%async_computation.7 | async-start | bytes 32768 | tf_op jit(solution)/shard_map/all_to_all | solution.py:76
  217.2 10.0 %all-to-all-start.8 = ((f32[8,8,128]{2,1,0:T(8,128)}), f32[8,8,128]{2,1,0:T(8,128)S(1)}, u32[]{:S(2)}, u32[]{:S(2)}) async-start(f32[8,8,128]{2,1,0:T(8,128)} %bitcast.66), calls=%async_computation.8 | async-start | bytes 65536 | tf_op jit(solution)/shard_map/all_to_all | solution.py:63
  229.1 38.0 %all-to-all-start.9 = ((bf16[8,8,128]{2,1,0:T(8,128)(2,1)}), bf16[8,8,128]{2,1,0:T(8,128)(2,1)S(1)}, u32[]{:S(2)}, u32[]{:S(2)}) async-start(bf16[8,8,128]{2,1,0:T(8,128)(2,1)} %bitcast.70), calls=%async_computation.9 | async-start | bytes 32768 | tf_op jit(solution)/shard_map/all_to_all | solution.py:76
  276.3 10.0 %all-to-all-start.10 = ((f32[8,8,128]{2,1,0:T(8,128)}), f32[8,8,128]{2,1,0:T(8,128)S(1)}, u32[]{:S(2)}, u32[]{:S(2)}) async-start(f32[8,8,128]{2,1,0:T(8,128)} %bitcast.79), calls=%async_computation.10 | async-start | bytes 65536 | tf_op jit(solution)/shard_map/all_to_all | solution.py:63
  288.2 38.6 %all-to-all-start.11 = ((bf16[8,8,128]{2,1,0:T(8,128)(2,1)}), bf16[8,8,128]{2,1,0:T(8,128)(2,1)S(1)}, u32[]{:S(2)}, u32[]{:S(2)}) async-start(bf16[8,8,128]{2,1,0:T(8,128)(2,1)} %bitcast.83), calls=%async_computation.11 | async-start | bytes 32768 | tf_op jit(solution)/shard_map/all_to_all | solution.py:76
  336.0 10.0 %all-to-all-start.13 = ((f32[8,8,128]{2,1,0:T(8,128)}), f32[8,8,128]{2,1,0:T(8,128)S(1)}, u32[]{:S(2)}, u32[]{:S(2)}) async-start(f32[8,8,128]{2,1,0:T(8,128)} %bitcast.98), calls=%async_computation.13 | async-start | bytes 65536 | tf_op jit(solution)/shard_map/all_to_all | solution.py:63
  345.9 10.3 %all-to-all-start.12 = ((f32[8,8,128]{2,1,0:T(8,128)}), f32[8,8,128]{2,1,0:T(8,128)S(1)}, u32[]{:S(2)}, u32[]{:S(2)}) async-start(f32[8,8,128]{2,1,0:T(8,128)} %bitcast.92), calls=%async_computation.12 | async-start | bytes 65536 | tf_op jit(solution)/shard_map/all_to_all | solution.py:63
where the time goes:
time: 358 us; the launch traced here: 357 us
  blocking collectives  193 us (54%)
  starting transfers between devices  51.1 us (14%)
  waiting for transfers between devices  47.8 us (13%)
  local copies, waits for them, and re-layouts  29 us (8%)
  between operations  14 us (4%)
  other arithmetic  11.6 us (3%)
  matrix products  10.6 us (3%)
    psum x5, blocking collectives, shards(): lax.psum((jnp.sum(primal_shift * primal_shift), jnp.sum(dual_shift * dual...  166 us
    all_to_all x7, waiting for transfers between devices, primal_product(): lax.all_to_all(outgoing, 'path', split_axis=0, concat_axis=0, tiled=True)  38.7 us
    all_to_all x7, starting transfers between devices, primal_product(): lax.all_to_all(outgoing, 'path', split_axis=0, concat_axis=0, tiled=True)  23.6 us
    all_to_all x6, starting transfers between devices, shards(): lax.all_to_all(replies, 'path', split_axis=0, concat_axis=0, tiled=True)  20.1 us
    unnamed x6, blocking collectives  14.8 us
    all_gather x7, blocking collectives, primal_product(): primal_low = lax.all_gather(primal_low, 'cons', axis=0, tiled=True)  12.4 us
    scatter x7, local copies, waits for them, and re-layouts, primal_product(): jnp.zeros((path_count * capacity, edge), jnp.float32).at[targets]  8.69 us
    all_to_all x1, starting transfers between devices, shards(): lax.all_to_all(slot_rows, 'path', split_axis=0, concat_axis=0, tiled=True)  7.41 us
  transfers between devices with their start and end apart: 14, of which 9 were waited for; matrix products, arithmetic and copies ran while one was open for 1% of the time, Pallas kernels for 0%

commit v1 on v0

--- a/solution.py
+++ b/solution.py
@@ -2,6 +2,17 @@
 import jax.numpy as jnp
 from jax import lax
 from jax.sharding import PartitionSpec as P
+
+
+def split_up(array, dim, size):
+    before, after = (array.shape[:dim], array.shape[dim + 1 :])
+    return jnp.moveaxis(array.reshape(*before, size, -1, *after), dim, 0)
+
+
+def joined_along(pieces, dim):
+    pieces = jnp.moveaxis(pieces, 0, dim)
+    shape = pieces.shape
+    return pieces.reshape(*shape[:dim], shape[dim] * shape[dim + 1], *shape[dim + 2 :])
 
 
 def tile_rows(tile_values, col_blocks, primal_low):
@@ -73,7 +84,14 @@
     for turn_index in range(restart_flags.shape[0]):
         dual_low = dual_now.astype(jnp.bfloat16)
         replies = dual_low.reshape(own_blocks, edge)[reply_rows]
-        returned = lax.all_to_all(replies, "path", split_axis=0, concat_axis=0, tiled=True)
+        peers, index = (lax.axis_size("path"), lax.axis_index("path"))
+        parts = split_up(replies, 0, peers)
+        gathered = [parts[index]]
+        for step in range(1, peers):
+            sent = parts[index ^ step]
+            gathered.append(lax.ppermute(sent, "path", [(i, i ^ step) for i in range(peers)]))
+        parts = jnp.stack(gathered)[index ^ jnp.arange(peers)]
+        returned = joined_along(parts, 0)
         picked = returned[targets]
         partial_terms = col_partial(tile_values, picked, col_blocks, col_count)
         gradient = lax.psum_scatter(partial_terms, "cons", scatter_dimension=0, tiled=True)

time: 358 us -> 409 us (1.14)
  starting transfers between devices: 51.1 us -> 94.8 us
  waiting for transfers between devices: 47.8 us -> 68.1 us
  blocking collectives: 193 us -> 178 us
    ppermute x0 -> x42, starting transfers between devices: none -> 53.4 us  [shards(): lax.ppermute(sent, 'path', [(i, i ^ step) for i in range(peers)])]
    ppermute x0 -> x42, waiting for transfers between devices: none -> 23.9 us  [shards(): lax.ppermute(sent, 'path', [(i, i ^ step) for i in range(peers)])]
    all_to_all x6 -> x0, starting transfers between devices: 20.1 us -> none  [shards(): lax.all_to_all(replies, 'path', split_axis=0, concat_axis=0, tiled=True)]
    psum x5, blocking collectives: 166 us -> 151 us  [shards(): lax.psum((jnp.sum(primal_shift * primal_shift), jnp.sum(dual_shift * dual...]
    all_to_all x7, starting transfers between devices: 23.6 us -> 34.1 us  [primal_product(): lax.all_to_all(outgoing, 'path', split_axis=0, concat_axis=0, tiled=True)]
  transfers between devices with their start and end apart: 14 -> 50, of which waited for: 9 -> 20; matrix products, arithmetic and copies ran while one was open for 1% -> 1% of each run, Pallas kernels for 0% -> 0%
where the time goes in v1:
time: 409 us; the launch traced here: 407 us
  blocking collectives  178 us (44%)
  starting transfers between devices  94.8 us (23%)
  waiting for transfers between devices  68.1 us (17%)
  local copies, waits for them, and re-layouts  30 us (7%)
  between operations  14.3 us (3%)
  other arithmetic  11.6 us (3%)
  matrix products  10.7 us (3%)
    psum x5, blocking collectives, shards(): lax.psum((jnp.sum(primal_shift * primal_shift), jnp.sum(dual_shift * dual...  151 us
    ppermute x42, starting transfers between devices, shards(): lax.ppermute(sent, 'path', [(i, i ^ step) for i in range(peers)])  53.4 us
    all_to_all x7, waiting for transfers between devices, primal_product(): lax.all_to_all(outgoing, 'path', split_axis=0, concat_axis=0, tiled=True)  39.1 us
    all_to_all x7, starting transfers between devices, primal_product(): lax.all_to_all(outgoing, 'path', split_axis=0, concat_axis=0, tiled=True)  34.1 us
    ppermute x42, waiting for transfers between devices, shards(): lax.ppermute(sent, 'path', [(i, i ^ step) for i in range(peers)])  23.9 us
    unnamed x6, blocking collectives  14.8 us
    all_gather x7, blocking collectives, primal_product(): primal_low = lax.all_gather(primal_low, 'cons', axis=0, tiled=True)  12.4 us
    scatter x7, local copies, waits for them, and re-layouts, primal_product(): jnp.zeros((path_count * capacity, edge), jnp.float32).at[targets]  8.69 us
  transfers between devices with their start and end apart: 50, of which 20 were waited for; matrix products, arithmetic and copies ran while one was open for 1% of the time, Pallas kernels for 0%

profile of v1, /device:TPU:0, one launch (start us, length us, event | category | flops | bytes accessed | tf_op | source)
XLA Modules:
  0.0 407.4 jit_solution(3274574257460727536)
XLA Ops:
  3.4 7.3 %all-to-all-start = ((s32[8,8,1]{1,2,0:T(1,128)}), s32[8,8,1]{1,2,0:T(1,128)S(1)}, u32[]{:S(2)}, u32[]{:S(2)}) async-start(s32[8,8,1]{1,2,0:T(1,128)} %bitcast.14), calls=%async_computation | async-start | bytes 8192 | tf_op jit(solution)/shard_map/all_to_all | solution.py:64
  12.0 5.1 %all-to-all-done = s32[8,8,1]{1,2,0:T(1,128)S(1)} async-done(((s32[8,8,1]{1,2,0:T(1,128)}), s32[8,8,1]{1,2,0:T(1,128)S(1)}, u32[]{:S(2)}, u32[]{:S(2)}) %all-to-all-start) | async-done | bytes 288 | tf_op jit(solution)/shard_map/all_to_all | solution.py:64
  45.5 5.4 %all-to-all-start.1 = ((f32[8,8,128]{2,1,0:T(8,128)}), f32[8,8,128]{2,1,0:T(8,128)S(1)}, u32[]{:S(2)}, u32[]{:S(2)}) async-start(f32[8,8,128]{2,1,0:T(8,128)} %bitcast.42), calls=%async_computation.1 | async-start | bytes 65536 | tf_op jit(solution)/shard_map/all_to_all | solution.py:74
  51.0 6.6 %all-to-all-done.1 = f32[8,8,128]{2,1,0:T(8,128)S(1)} async-done(((f32[8,8,128]{2,1,0:T(8,128)}), f32[8,8,128]{2,1,0:T(8,128)S(1)}, u32[]{:S(2)}, u32[]{:S(2)}) %all-to-all-start.1) | async-done | bytes 32800 | tf_op jit(solution)/shard_map/all_to_all | solution.py:74
  61.0 30.0 %all-reduce.10 = (f32[]{:T(128)}, f32[]{:T(128)}) all-reduce(f32[]{:T(128)} %get-tuple-element.88, f32[]{:T(128)} %get-tuple-element.33), channel_id=1, replica_groups=mesh['groups'=2,'path'=8,'cons'=2] {'path','cons'}, use_global_device_ids=true, to_apply=%region_6.7 | all-reduce | flops 2 | bytes 16 | tf_op jit(solution)/shard_map/psum | solution.py:109
  92.5 5.7 %collective-permute-start.11 = (bf16[8,128]{1,0:T(8,128)(2,1)S(1)}, bf16[8,128]{1,0:T(8,128)(2,1)S(1)}, u32[]{:S(2)}, u32[]{:S(2)}) collective-permute-start(bf16[8,128]{1,0:T(8,128)(2,1)S(1)} %get-tuple-element.70), channel_id=1, source_target_pairs={{0,10},{2,8},{4,14},{6,12},{8,2},{10,0},{12,6},{14,4},{1,11},{3,9}... | collective-permute-start | bytes 6152 | tf_op jit(solution)/shard_map/ppermute | solution.py:92
  114.5 5.0 %all-to-all-start.2 = ((f32[8,8,128]{2,1,0:T(8,128)}), f32[8,8,128]{2,1,0:T(8,128)S(1)}, u32[]{:S(2)}, u32[]{:S(2)}) async-start(f32[8,8,128]{2,1,0:T(8,128)} %bitcast.69), calls=%async_computation.2 | async-start | bytes 65536 | tf_op jit(solution)/shard_map/all_to_all | solution.py:74
  120.2 6.0 %all-to-all-done.2 = f32[8,8,128]{2,1,0:T(8,128)S(1)} async-done(((f32[8,8,128]{2,1,0:T(8,128)}), f32[8,8,128]{2,1,0:T(8,128)S(1)}, u32[]{:S(2)}, u32[]{:S(2)}) %all-to-all-start.2) | async-done | bytes 32800 | tf_op jit(solution)/shard_map/all_to_all | solution.py:74
  128.2 30.2 %all-reduce.9 = (f32[]{:T(128)}, f32[]{:T(128)}) all-reduce(f32[]{:T(128)} %get-tuple-element.31, f32[]{:T(128)} %get-tuple-element.29), channel_id=1, replica_groups=mesh['groups'=2,'path'=8,'cons'=2] {'path','cons'}, use_global_device_ids=true, to_apply=%region_13.14 | all-reduce | flops 2 | bytes 16 | tf_op jit(solution)/shard_map/psum | solution.py:109
  160.0 5.7 %collective-permute-start.18 = (bf16[8,128]{1,0:T(8,128)(2,1)S(1)}, bf16[8,128]{1,0:T(8,128)(2,1)S(1)}, u32[]{:S(2)}, u32[]{:S(2)}) collective-permute-start(bf16[8,128]{1,0:T(8,128)(2,1)S(1)} %get-tuple-element.62), channel_id=1, source_target_pairs={{0,10},{2,8},{4,14},{6,12},{8,2},{10,0},{12,6},{14,4},{1,11},{3,9}... | collective-permute-start | bytes 6152 | tf_op jit(solution)/shard_map/ppermute | solution.py:92
  182.0 5.0 %all-to-all-start.3 = ((f32[8,8,128]{2,1,0:T(8,128)}), f32[8,8,128]{2,1,0:T(8,128)S(1)}, u32[]{:S(2)}, u32[]{:S(2)}) async-start(f32[8,8,128]{2,1,0:T(8,128)} %bitcast.96), calls=%async_computation.3 | async-start | bytes 65536 | tf_op jit(solution)/shard_map/all_to_all | solution.py:74
  187.7 6.0 %all-to-all-done.3 = f32[8,8,128]{2,1,0:T(8,128)S(1)} async-done(((f32[8,8,128]{2,1,0:T(8,128)}), f32[8,8,128]{2,1,0:T(8,128)S(1)}, u32[]{:S(2)}, u32[]{:S(2)}) %all-to-all-start.3) | async-done | bytes 32800 | tf_op jit(solution)/shard_map/all_to_all | solution.py:74
  195.7 30.1 %all-reduce.8 = (f32[]{:T(128)}, f32[]{:T(128)}) all-reduce(f32[]{:T(128)} %get-tuple-element.25, f32[]{:T(128)} %get-tuple-element.21), channel_id=1, replica_groups=mesh['groups'=2,'path'=8,'cons'=2] {'path','cons'}, use_global_device_ids=true, to_apply=%region_20.21 | all-reduce | flops 2 | bytes 16 | tf_op jit(solution)/shard_map/psum | solution.py:109
  227.4 5.7 %collective-permute-start.25 = (bf16[8,128]{1,0:T(8,128)(2,1)S(1)}, bf16[8,128]{1,0:T(8,128)(2,1)S(1)}, u32[]{:S(2)}, u32[]{:S(2)}) collective-permute-start(bf16[8,128]{1,0:T(8,128)(2,1)S(1)} %get-tuple-element.54), channel_id=1, source_target_pairs={{0,10},{2,8},{4,14},{6,12},{8,2},{10,0},{12,6},{14,4},{1,11},{3,9}... | collective-permute-start | bytes 6152 | tf_op jit(solution)/shard_map/ppermute | solution.py:92
  249.3 5.0 %all-to-all-start.4 = ((f32[8,8,128]{2,1,0:T(8,128)}), f32[8,8,128]{2,1,0:T(8,128)S(1)}, u32[]{:S(2)}, u32[]{:S(2)}) async-start(f32[8,8,128]{2,1,0:T(8,128)} %bitcast.123), calls=%async_computation.4 | async-start | bytes 65536 | tf_op jit(solution)/shard_map/all_to_all | solution.py:74
  255.0 6.0 %all-to-all-done.4 = f32[8,8,128]{2,1,0:T(8,128)S(1)} async-done(((f32[8,8,128]{2,1,0:T(8,128)}), f32[8,8,128]{2,1,0:T(8,128)S(1)}, u32[]{:S(2)}, u32[]{:S(2)}) %all-to-all-start.4) | async-done | bytes 32800 | tf_op jit(solution)/shard_map/all_to_all | solution.py:74
  263.0 30.1 %all-reduce.7 = (f32[]{:T(128)}, f32[]{:T(128)}) all-reduce(f32[]{:T(128)} %get-tuple-element.19, f32[]{:T(128)} %get-tuple-element.17), channel_id=1, replica_groups=mesh['groups'=2,'path'=8,'cons'=2] {'path','cons'}, use_global_device_ids=true, to_apply=%region_27.28 | all-reduce | flops 2 | bytes 16 | tf_op jit(solution)/shard_map/psum | solution.py:109
  294.8 5.7 %collective-permute-start.32 = (bf16[8,128]{1,0:T(8,128)(2,1)S(1)}, bf16[8,128]{1,0:T(8,128)(2,1)S(1)}, u32[]{:S(2)}, u32[]{:S(2)}) collective-permute-start(bf16[8,128]{1,0:T(8,128)(2,1)S(1)} %get-tuple-element.46), channel_id=1, source_target_pairs={{0,10},{2,8},{4,14},{6,12},{8,2},{10,0},{12,6},{14,4},{1,11},{3,9}... | collective-permute-start | bytes 6152 | tf_op jit(solution)/shard_map/ppermute | solution.py:92
  316.7 5.0 %all-to-all-start.5 = ((f32[8,8,128]{2,1,0:T(8,128)}), f32[8,8,128]{2,1,0:T(8,128)S(1)}, u32[]{:S(2)}, u32[]{:S(2)}) async-start(f32[8,8,128]{2,1,0:T(8,128)} %bitcast.150), calls=%async_computation.5 | async-start | bytes 65536 | tf_op jit(solution)/shard_map/all_to_all | solution.py:74
  322.3 6.0 %all-to-all-done.5 = f32[8,8,128]{2,1,0:T(8,128)S(1)} async-done(((f32[8,8,128]{2,1,0:T(8,128)}), f32[8,8,128]{2,1,0:T(8,128)S(1)}, u32[]{:S(2)}, u32[]{:S(2)}) %all-to-all-start.5) | async-done | bytes 32800 | tf_op jit(solution)/shard_map/all_to_all | solution.py:74
  331.0 30.1 %all-reduce.6 = (f32[]{:T(128)}, f32[]{:T(128)}) all-reduce(f32[]{:T(128)} %get-tuple-element.86, f32[]{:T(128)} %get-tuple-element.84), channel_id=1, replica_groups=mesh['groups'=2,'path'=8,'cons'=2] {'path','cons'}, use_global_device_ids=true, to_apply=%region_34.35 | all-reduce | flops 2 | bytes 16 | tf_op jit(solution)/shard_map/psum | solution.py:109
  362.8 5.7 %collective-permute-start.39 = (bf16[8,128]{1,0:T(8,128)(2,1)S(1)}, bf16[8,128]{1,0:T(8,128)(2,1)S(1)}, u32[]{:S(2)}, u32[]{:S(2)}) collective-permute-start(bf16[8,128]{1,0:T(8,128)(2,1)S(1)} %get-tuple-element.38), channel_id=1, source_target_pairs={{0,10},{2,8},{4,14},{6,12},{8,2},{10,0},{12,6},{14,4},{1,11},{3,9}... | collective-permute-start | bytes 6152 | tf_op jit(solution)/shard_map/ppermute | solution.py:92
  384.7 5.0 %all-to-all-start.7 = ((f32[8,8,128]{2,1,0:T(8,128)}), f32[8,8,128]{2,1,0:T(8,128)S(1)}, u32[]{:S(2)}, u32[]{:S(2)}) async-start(f32[8,8,128]{2,1,0:T(8,128)} %bitcast.183), calls=%async_computation.7 | async-start | bytes 65536 | tf_op jit(solution)/shard_map/all_to_all | solution.py:74
  400.7 6.0 %all-to-all-done.6 = f32[8,8,128]{2,1,0:T(8,128)S(1)} async-done(((f32[8,8,128]{2,1,0:T(8,128)}), f32[8,8,128]{2,1,0:T(8,128)S(1)}, u32[]{:S(2)}, u32[]{:S(2)}) %all-to-all-start.6) | async-done | bytes 32800 | tf_op jit(solution)/shard_map/all_to_all | solution.py:74
  (273 shorter events, 134.5 us)
Async XLA Ops:
  3.4 13.7 %all-to-all-start = ((s32[8,8,1]{1,2,0:T(1,128)}), s32[8,8,1]{1,2,0:T(1,128)S(1)}, u32[]{:S(2)}, u32[]{:S(2)}) async-start(s32[8,8,1]{1,2,0:T(1,128)} %bitcast.14), calls=%async_computation | async-start | bytes 8192 | tf_op jit(solution)/shard_map/all_to_all | solution.py:64
  19.1 9.8 %collective-permute-start = (bf16[8,128]{1,0:T(8,128)(2,1)S(1)}, bf16[8,128]{1,0:T(8,128)(2,1)S(1)}, u32[]{:S(2)}, u32[]{:S(2)}) collective-permute-start(bf16[8,128]{1,0:T(8,128)(2,1)S(1)} %get-tuple-element.82), channel_id=1, source_target_pairs={{0,2},{2,0},{4,6},{6,4},{8,10},{10,8},{12,14},{14,12},{1,3},{3,1},... | collective-permute-start | bytes 6152 | tf_op jit(solution)/shard_map/ppermute | solution.py:92
  23.6 10.0 %collective-permute-start.2 = (bf16[8,128]{1,0:T(8,128)(2,1)S(1)}, bf16[8,128]{1,0:T(8,128)(2,1)S(1)}, u32[]{:S(2)}, u32[]{:S(2)}) collective-permute-start(bf16[8,128]{1,0:T(8,128)(2,1)S(1)} %get-tuple-element.80), channel_id=1, source_target_pairs={{0,6},{2,4},{4,2},{6,0},{8,14},{10,12},{12,10},{14,8},{1,7},{3,5},... | collective-permute-start | bytes 6152 | tf_op jit(solution)/shard_map/ppermute | solution.py:92
  45.5 12.1 %all-to-all-start.1 = ((f32[8,8,128]{2,1,0:T(8,128)}), f32[8,8,128]{2,1,0:T(8,128)S(1)}, u32[]{:S(2)}, u32[]{:S(2)}) async-start(f32[8,8,128]{2,1,0:T(8,128)} %bitcast.42), calls=%async_computation.1 | async-start | bytes 65536 | tf_op jit(solution)/shard_map/all_to_all | solution.py:74
  59.1 39.1 %collective-permute-start.7 = (bf16[8,128]{1,0:T(8,128)(2,1)S(1)}, bf16[8,128]{1,0:T(8,128)(2,1)S(1)}, u32[]{:S(2)}, u32[]{:S(2)}) collective-permute-start(bf16[8,128]{1,0:T(8,128)(2,1)S(1)} %get-tuple-element.74), channel_id=1, source_target_pairs={{0,2},{2,0},{4,6},{6,4},{8,10},{10,8},{12,14},{14,12},{1,3},{3,1},... | collective-permute-start | bytes 6152 | tf_op jit(solution)/shard_map/ppermute | solution.py:92
  92.4 7.9 %collective-permute-start.9 = (bf16[8,128]{1,0:T(8,128)(2,1)S(1)}, bf16[8,128]{1,0:T(8,128)(2,1)S(1)}, u32[]{:S(2)}, u32[]{:S(2)}) collective-permute-start(bf16[8,128]{1,0:T(8,128)(2,1)S(1)} %get-tuple-element.72), channel_id=1, source_target_pairs={{0,6},{2,4},{4,2},{6,0},{8,14},{10,12},{12,10},{14,8},{1,7},{3,5},... | collective-permute-start | bytes 6152 | tf_op jit(solution)/shard_map/ppermute | solution.py:92
  92.5 7.9 %collective-permute-start.10 = (bf16[8,128]{1,0:T(8,128)(2,1)S(1)}, bf16[8,128]{1,0:T(8,128)(2,1)S(1)}, u32[]{:S(2)}, u32[]{:S(2)}) collective-permute-start(bf16[8,128]{1,0:T(8,128)(2,1)S(1)} %get-tuple-element.71), channel_id=1, source_target_pairs={{0,8},{2,10},{4,12},{6,14},{8,0},{10,2},{12,4},{14,6},{1,9},{3,11}... | collective-permute-start | bytes 6152 | tf_op jit(solution)/shard_map/ppermute | solution.py:92
  114.5 11.7 %all-to-all-start.2 = ((f32[8,8,128]{2,1,0:T(8,128)}), f32[8,8,128]{2,1,0:T(8,128)S(1)}, u32[]{:S(2)}, u32[]{:S(2)}) async-start(f32[8,8,128]{2,1,0:T(8,128)} %bitcast.69), calls=%async_computation.2 | async-start | bytes 65536 | tf_op jit(solution)/shard_map/all_to_all | solution.py:74
  127.6 38.1 %collective-permute-start.14 = (bf16[8,128]{1,0:T(8,128)(2,1)S(1)}, bf16[8,128]{1,0:T(8,128)(2,1)S(1)}, u32[]{:S(2)}, u32[]{:S(2)}) collective-permute-start(bf16[8,128]{1,0:T(8,128)(2,1)S(1)} %get-tuple-element.66), channel_id=1, source_target_pairs={{0,2},{2,0},{4,6},{6,4},{8,10},{10,8},{12,14},{14,12},{1,3},{3,1},... | collective-permute-start | bytes 6152 | tf_op jit(solution)/shard_map/ppermute | solution.py:92
  159.8 7.9 %collective-permute-start.16 = (bf16[8,128]{1,0:T(8,128)(2,1)S(1)}, bf16[8,128]{1,0:T(8,128)(2,1)S(1)}, u32[]{:S(2)}, u32[]{:S(2)}) collective-permute-start(bf16[8,128]{1,0:T(8,128)(2,1)S(1)} %get-tuple-element.64), channel_id=1, source_target_pairs={{0,6},{2,4},{4,2},{6,0},{8,14},{10,12},{12,10},{14,8},{1,7},{3,5},... | collective-permute-start | bytes 6152 | tf_op jit(solution)/shard_map/ppermute | solution.py:92
  159.9 7.9 %collective-permute-start.17 = (bf16[8,128]{1,0:T(8,128)(2,1)S(1)}, bf16[8,128]{1,0:T(8,128)(2,1)S(1)}, u32[]{:S(2)}, u32[]{:S(2)}) collective-permute-start(bf16[8,128]{1,0:T(8,128)(2,1)S(1)} %get-tuple-element.63), channel_id=1, source_target_pairs={{0,8},{2,10},{4,12},{6,14},{8,0},{10,2},{12,4},{14,6},{1,9},{3,11}... | collective-permute-start | bytes 6152 | tf_op jit(solution)/shard_map/ppermute | solution.py:92
  182.0 11.7 %all-to-all-start.3 = ((f32[8,8,128]{2,1,0:T(8,128)}), f32[8,8,128]{2,1,0:T(8,128)S(1)}, u32[]{:S(2)}, u32[]{:S(2)}) async-start(f32[8,8,128]{2,1,0:T(8,128)} %bitcast.96), calls=%async_computation.3 | async-start | bytes 65536 | tf_op jit(solution)/shard_map/all_to_all | solution.py:74
  195.1 38.0 %collective-permute-start.21 = (bf16[8,128]{1,0:T(8,128)(2,1)S(1)}, bf16[8,128]{1,0:T(8,128)(2,1)S(1)}, u32[]{:S(2)}, u32[]{:S(2)}) collective-permute-start(bf16[8,128]{1,0:T(8,128)(2,1)S(1)} %get-tuple-element.58), channel_id=1, source_target_pairs={{0,2},{2,0},{4,6},{6,4},{8,10},{10,8},{12,14},{14,12},{1,3},{3,1},... | collective-permute-start | bytes 6152 | tf_op jit(solution)/shard_map/ppermute | solution.py:92
  227.3 7.9 %collective-permute-start.23 = (bf16[8,128]{1,0:T(8,128)(2,1)S(1)}, bf16[8,128]{1,0:T(8,128)(2,1)S(1)}, u32[]{:S(2)}, u32[]{:S(2)}) collective-permute-start(bf16[8,128]{1,0:T(8,128)(2,1)S(1)} %get-tuple-element.56), channel_id=1, source_target_pairs={{0,6},{2,4},{4,2},{6,0},{8,14},{10,12},{12,10},{14,8},{1,7},{3,5},... | collective-permute-start | bytes 6152 | tf_op jit(solution)/shard_map/ppermute | solution.py:92
  227.3 7.9 %collective-permute-start.24 = (bf16[8,128]{1,0:T(8,128)(2,1)S(1)}, bf16[8,128]{1,0:T(8,128)(2,1)S(1)}, u32[]{:S(2)}, u32[]{:S(2)}) collective-permute-start(bf16[8,128]{1,0:T(8,128)(2,1)S(1)} %get-tuple-element.55), channel_id=1, source_target_pairs={{0,8},{2,10},{4,12},{6,14},{8,0},{10,2},{12,4},{14,6},{1,9},{3,11}... | collective-permute-start | bytes 6152 | tf_op jit(solution)/shard_map/ppermute | solution.py:92
  249.3 11.7 %all-to-all-start.4 = ((f32[8,8,128]{2,1,0:T(8,128)}), f32[8,8,128]{2,1,0:T(8,128)S(1)}, u32[]{:S(2)}, u32[]{:S(2)}) async-start(f32[8,8,128]{2,1,0:T(8,128)} %bitcast.123), calls=%async_computation.4 | async-start | bytes 65536 | tf_op jit(solution)/shard_map/all_to_all | solution.py:74
  262.5 38.0 %collective-permute-start.28 = (bf16[8,128]{1,0:T(8,128)(2,1)S(1)}, bf16[8,128]{1,0:T(8,128)(2,1)S(1)}, u32[]{:S(2)}, u32[]{:S(2)}) collective-permute-start(bf16[8,128]{1,0:T(8,128)(2,1)S(1)} %get-tuple-element.50), channel_id=1, source_target_pairs={{0,2},{2,0},{4,6},{6,4},{8,10},{10,8},{12,14},{14,12},{1,3},{3,1},... | collective-permute-start | bytes 6152 | tf_op jit(solution)/shard_map/ppermute | solution.py:92
  294.6 7.9 %collective-permute-start.30 = (bf16[8,128]{1,0:T(8,128)(2,1)S(1)}, bf16[8,128]{1,0:T(8,128)(2,1)S(1)}, u32[]{:S(2)}, u32[]{:S(2)}) collective-permute-start(bf16[8,128]{1,0:T(8,128)(2,1)S(1)} %get-tuple-element.48), channel_id=1, source_target_pairs={{0,6},{2,4},{4,2},{6,0},{8,14},{10,12},{12,10},{14,8},{1,7},{3,5},... | collective-permute-start | bytes 6152 | tf_op jit(solution)/shard_map/ppermute | solution.py:92
  294.7 7.9 %collective-permute-start.31 = (bf16[8,128]{1,0:T(8,128)(2,1)S(1)}, bf16[8,128]{1,0:T(8,128)(2,1)S(1)}, u32[]{:S(2)}, u32[]{:S(2)}) collective-permute-start(bf16[8,128]{1,0:T(8,128)(2,1)S(1)} %get-tuple-element.47), channel_id=1, source_target_pairs={{0,8},{2,10},{4,12},{6,14},{8,0},{10,2},{12,4},{14,6},{1,9},{3,11}... | collective-permute-start | bytes 6152 | tf_op jit(solution)/shard_map/ppermute | solution.py:92
  316.7 11.7 %all-to-all-start.5 = ((f32[8,8,128]{2,1,0:T(8,128)}), f32[8,8,128]{2,1,0:T(8,128)S(1)}, u32[]{:S(2)}, u32[]{:S(2)}) async-start(f32[8,8,128]{2,1,0:T(8,128)} %bitcast.150), calls=%async_computation.5 | async-start | bytes 65536 | tf_op jit(solution)/shard_map/all_to_all | solution.py:74
  329.8 38.7 %collective-permute-start.35 = (bf16[8,128]{1,0:T(8,128)(2,1)S(1)}, bf16[8,128]{1,0:T(8,128)(2,1)S(1)}, u32[]{:S(2)}, u32[]{:S(2)}) collective-permute-start(bf16[8,128]{1,0:T(8,128)(2,1)S(1)} %get-tuple-element.42), channel_id=1, source_target_pairs={{0,2},{2,0},{4,6},{6,4},{8,10},{10,8},{12,14},{14,12},{1,3},{3,1},... | collective-permute-start | bytes 6152 | tf_op jit(solution)/shard_map/ppermute | solution.py:92
  362.6 7.9 %collective-permute-start.37 = (bf16[8,128]{1,0:T(8,128)(2,1)S(1)}, bf16[8,128]{1,0:T(8,128)(2,1)S(1)}, u32[]{:S(2)}, u32[]{:S(2)}) collective-permute-start(bf16[8,128]{1,0:T(8,128)(2,1)S(1)} %get-tuple-element.40), channel_id=1, source_target_pairs={{0,6},{2,4},{4,2},{6,0},{8,14},{10,12},{12,10},{14,8},{1,7},{3,5},... | collective-permute-start | bytes 6152 | tf_op jit(solution)/shard_map/ppermute | solution.py:92
  384.7 11.7 %all-to-all-start.7 = ((f32[8,8,128]{2,1,0:T(8,128)}), f32[8,8,128]{2,1,0:T(8,128)S(1)}, u32[]{:S(2)}, u32[]{:S(2)}) async-start(f32[8,8,128]{2,1,0:T(8,128)} %bitcast.183), calls=%async_computation.7 | async-start | bytes 65536 | tf_op jit(solution)/shard_map/all_to_all | solution.py:74
  396.4 10.3 %all-to-all-start.6 = ((f32[8,8,128]{2,1,0:T(8,128)}), f32[8,8,128]{2,1,0:T(8,128)S(1)}, u32[]{:S(2)}, u32[]{:S(2)}) async-start(f32[8,8,128]{2,1,0:T(8,128)} %bitcast.177), calls=%async_computation.6 | async-start | bytes 65536 | tf_op jit(solution)/shard_map/all_to_all | solution.py:74
  (36 other events, 223.0 us)
